TPU v7x, 32 devices: a whole 2x2x4 slice. The times are simulated.
32 devices in a mesh: seq: 16 (over z, y, x), doc: 2 (over core).
Axes of the slice: x: 2, y: 2, z: 4, core: 2. Of those that a mesh axis runs over, the one named last changes fastest.
Arguments:
- conv_input: bfloat16 [4096, 4352], P(('doc', 'seq')), parts along dimension 0, may hold values from -6 to 6
- gate_input: bfloat16 [4096, 4096], P(('doc', 'seq')), parts along dimension 0, may hold values from -6 to 6
- step_input: bfloat16 [4096, 64], P(('doc', 'seq')), parts along dimension 0, may hold values from -1.1 to 2.9
- conv_weight: float32 [4, 4352], replicated, may hold values from -3 to 3
- convolution_bias: float32 [4352], replicated, may hold values from -0.5 to 0.5
- step_bias: float32 [64], replicated, may hold values from -12 to -2, as said below
- decay_log: float32 [64], replicated, may hold values from -3.3 to -1, as said below
- skip_gain: float32 [64], replicated, may hold values from 0.5 to 2
- norm_gain: float32 [4096], replicated, may hold values from 0.5 to 1.5
Outputs:
- normed: bfloat16 [4096, 4096], P(('doc', 'seq')), parts along dimension 0
There are 2 independent parts, one for each index of `doc`. A program takes and returns all parts, laid end to end along the dimension named above; an argument that names none is the same for every part. Nothing has to cross between parts.
Inputs may be any that keep to these rules, and one draw needn't show every extreme that they name: `decay_log`: one value a head. `step_bias`: one value a head.
All inputs are finite; a program needn't handle non-finite values.
Results may differ from a plain program's by a relative error of at most 0.0051.
Values may be sent and summed in bfloat16 or wider, within the bound.
A program may use at most 64 MiB of HBM per device.

v0:
```python
import jax
import jax.numpy as jnp
from jax import lax
from jax.sharding import PartitionSpec as P

HEADDIM = 64
STATE = 128
HEADS = 64
STRETCH = 256


def shifted(value, axis, steps):
    count = lax.axis_size(axis)
    initial, last = (max(0, -steps), min(count, count - steps))
    return lax.ppermute(value, axis, [(source, source + steps) for source in range(initial, last)])


def gated_norm(mixed_out, gate_input, norm_gain):
    gated = mixed_out.astype(jnp.float32) * jax.nn.silu(gate_input.astype(jnp.float32))
    spread = jnp.mean(gated * gated, axis=-1, keepdims=True)
    return (gated * lax.rsqrt(spread + 1e-05) * norm_gain[None, :]).astype(jnp.bfloat16)


def convolve(conv_input, conv_weight, convolution_bias):
    tap_count = conv_weight.shape[0]
    row_count = conv_input.shape[0]
    earlier = shifted(conv_input[row_count - (tap_count - 1) :], "seq", 1)
    padded = jnp.concatenate([earlier, conv_input], axis=0).astype(jnp.float32)
    mixed = convolution_bias[None, :]
    for offset in range(tap_count):
        mixed = mixed + conv_weight[offset][None, :] * padded[offset : offset + row_count]
    return jax.nn.silu(mixed).astype(jnp.bfloat16)


def dual_form(values, step_size, decay_rate, b_rows, c_rows, block_len):
    highest = lax.Precision.HIGHEST
    row_count, head_count, head_width = values.shape
    state_width = b_rows.shape[1]
    blocks = row_count // block_len
    block_values = values.reshape(blocks, block_len, head_count, head_width)
    block_step_sizes = step_size.reshape(blocks, block_len, head_count)
    block_b = b_rows.reshape(blocks, block_len, state_width)
    block_c = c_rows.reshape(blocks, block_len, state_width)
    within = jnp.cumsum(block_step_sizes * decay_rate[None, None, :], axis=1)
    ends = within[:, -1, :]
    totals = jnp.cumsum(ends, axis=0)
    before = totals - ends
    lower = jnp.arange(block_len)[:, None] >= jnp.arange(block_len)[None, :]
    turned = jnp.transpose(within, (0, 2, 1))
    diffs = jnp.where(lower[None, None], turned[:, :, :, None] - turned[:, :, None, :], -jnp.inf)
    scores = jnp.einsum("ctn,csn->cts", block_c, block_b, precision=highest)
    mixing = (
        jnp.exp(diffs) * scores[:, None] * jnp.transpose(block_step_sizes, (0, 2, 1))[:, :, None, :]
    )
    inside = jnp.einsum("chts,cshp->cthp", mixing, block_values, precision=highest)
    tail = jnp.exp(ends[:, None, :] - within) * block_step_sizes
    weighted = tail[:, :, :, None] * block_values
    states = jnp.einsum("cshp,csn->chpn", weighted, block_b, precision=highest)
    order = jnp.arange(blocks)
    earlier_mask = order[:, None] > order[None, :]
    gap = jnp.where(earlier_mask[None], before.T[:, :, None] - totals.T[:, None, :], -jnp.inf)
    entering = jnp.einsum("hcd,dhpn->chpn", jnp.exp(gap), states, precision=highest)
    outside = jnp.exp(within)[:, :, :, None] * jnp.einsum(
        "ctn,chpn->cthp", block_c, entering, precision=highest
    )
    result = (inside + outside).reshape(row_count, head_count, head_width)
    last = totals[-1]
    final = jnp.einsum("dh,dhpn->hpn", jnp.exp(last[None, :] - totals), states, precision=highest)
    decay_sum = (before[:, None, :] + within).reshape(row_count, head_count)
    return (result, final, decay_sum, last)


def shards(
    conv_input,
    gate_input,
    step_input,
    conv_weight,
    convolution_bias,
    step_bias,
    decay_log,
    skip_gain,
    norm_gain,
):
    inner_width = HEADS * HEADDIM
    decay_rate = -jnp.exp(decay_log)
    activated = convolve(conv_input, conv_weight, convolution_bias)
    head_values, head_steps = (
        lax.all_to_all(activated[:, :inner_width], "seq", split_axis=1, concat_axis=0, tiled=True),
        lax.all_to_all(step_input, "seq", split_axis=1, concat_axis=0, tiled=True),
    )
    shared = lax.all_gather(activated[:, inner_width:], "seq", axis=0, tiled=True)
    full_rows = shared.shape[0]
    own_heads = head_steps.shape[1]
    first_head = lax.axis_index("seq") * own_heads
    own_bias = lax.dynamic_slice_in_dim(step_bias, first_head, own_heads)
    own_rate = lax.dynamic_slice_in_dim(decay_rate, first_head, own_heads)
    own_skip = lax.dynamic_slice_in_dim(skip_gain, first_head, own_heads)
    values = head_values.astype(jnp.float32).reshape(full_rows, own_heads, HEADDIM)
    shared_rows = shared.astype(jnp.float32)
    step_size = jax.nn.softplus(head_steps.astype(jnp.float32) + own_bias[None, :])
    result, final, decay_sum, last = dual_form(
        values,
        step_size,
        own_rate,
        shared_rows[:, :STATE],
        shared_rows[:, STATE:],
        min(STRETCH, full_rows),
    )
    result = result + own_skip[None, :, None] * values
    head_output = result.astype(jnp.bfloat16).reshape(full_rows, own_heads * HEADDIM)
    mixed_out = lax.all_to_all(head_output, "seq", split_axis=0, concat_axis=1, tiled=True)
    return gated_norm(mixed_out, gate_input, norm_gain)


def solution(mesh):
    in_specs = (
        P(("doc", "seq"), None),
        P(("doc", "seq"), None),
        P(("doc", "seq"), None),
        P(),
        P(),
        P(),
        P(),
        P(),
        P(),
    )
    out_specs = P(("doc", "seq"), None)
    return jax.shard_map(shards, mesh=mesh, in_specs=in_specs, out_specs=out_specs, check_vma=False)
```

profile of v0, /device:TPU:0, one launch (start us, length us, event | category | flops | bytes accessed | tf_op | source)
XLA Modules:
  0.0 146.6 jit_solution(9924083408817625690)
XLA Ops:
  6.5 0.0 copy-start.3
  6.5 8.4 %all-to-all-start.1 = ((bf16[128,16,4]{0,2,1:T(4,128)(2,1)}), bf16[128,16,4]{0,2,1:T(4,128)(2,1)S(1)}, u32[]{:S(2)}, u32[]{:S(2)}) async-start(bf16[128,16,4]{0,2,1:T(4,128)(2,1)} %bitcast.77), calls=%async_computation.1 | async-start | bytes 32768 | tf_op jit(solution)/shard_map/all_to_all | solution.py:89
  15.0 0.0 all-gather.2.cloned.1.call-start
  15.0 0.9 slice.49
  15.9 3.8 %collective-permute-start = (bf16[3,4352]{1,0:T(4,128)(2,1)S(1)}, bf16[3,4352]{1,0:T(4,128)(2,1)S(1)}, u32[]{:S(2)}, u32[]{:S(2)}) collective-permute-start(bf16[3,4352]{1,0:T(4,128)(2,1)S(1)} %slice.49), channel_id=1, source_target_pairs={{0,2},{2,4},{4,6},{6,8},{8,10},{10,12},{12,14},{14,16},{16,18},{18... | collective-permute-start | bytes 78344 | tf_op jit(solution)/shard_map/ppermute | solution.py:15
  19.8 1.2 slice_reduce_fusion.4
  21.0 1.7 %copy.46 = bf16[128,4352]{0,1:T(8,128)(2,1)S(1)} copy(bf16[128,4352]{1,0:T(8,128)(2,1)} %param.9) | data formatting | bytes 2228224 | tf_op args[0]
  22.7 0.0 copy-done.3
  22.7 0.1 dynamic_slice.9
  22.8 0.0 collective-permute-done
  22.8 0.5 copy.45
  23.3 0.0 copy-start.1
  23.3 0.8 maximum_convert_fusion
  24.2 0.0 copy-done.1
  24.2 5.5 %multiply_convert_fusion = bf16[128,4352]{0,1:T(8,128)(2,1)S(1)} fusion(f32[131,4352]{0,1:T(8,128)S(1)} %maximum_convert_fusion, f32[4352]{0:T(1024)S(1)} %get-tuple-element.7, f32[4352]{0:T(1024)S(1)} %get-tuple-element.8, f32[4352]{0:T(1024)S(1)} %get-tuple-element.6, f32[4352]{0:T(1024)S(1)} %get-tuple-element.5, f32[4352]{0:T(1024)S(1)} %copy-done.1), kind=kLoop, calls=%fused_computation.23 | loop fusion | flops 7241728 | bytes 10114048 | tf_op jit(solution)/shard_map/convert_element_type | solution.py:32
  29.7 0.0 copy-start.4
  29.7 0.0 copy-start.5
  29.7 1.0 slice.68
  30.8 0.6 slice.71
  31.4 0.0 all-gather.2.cloned.1.call-update
  31.4 0.0 all-to-all-done.1
  31.4 5.9 %all-to-all-start = ((bf16[128,16,256]{0,2,1:T(8,128)(2,1)}), bf16[128,16,256]{0,2,1:T(8,128)(2,1)S(1)}, u32[]{:S(2)}, u32[]{:S(2)}) async-start(bf16[128,16,256]{0,2,1:T(8,128)(2,1)} %bitcast), calls=%async_computation | async-start | bytes 2097152 | tf_op jit(solution)/shard_map/all_to_all | solution.py:88
  37.3 0.0 copy-done.4
  37.3 0.1 dynamic_slice.10
  37.4 0.0 copy-done.5
  37.4 0.1 dynamic_slice.11
  37.5 0.1 mul.155
  37.6 0.1 mul.156
  37.7 0.1 multiply_bitcast_fusion
  37.8 2.3 %reduce-window.6 = f32[8,4,2,128]{3,0,1,2:T(8,128)S(1)} reduce-window(f32[8,4,2,128]{3,0,1,2:T(8,128)S(1)} %copy.49, f32[]{:T(128)} %constant.30.clone.1), window={size=1x1x1x128 pad=0_0x0_0x0_0x127_0}, to_apply=%region_0.1 | reduce-window | flops 1040384 | bytes 65540 | tf_op jit(solution)/shard_map/reduce-window
  40.1 0.2 slice_reduce_fusion
  40.3 0.1 copy_bitcast_fusion
  40.4 0.2 slice_reduce_fusion.5
  40.5 0.2 reduce_window_sum.36
  40.7 0.1 fusion.40
  40.9 21.0 %all-to-all-done = bf16[128,16,256]{0,2,1:T(8,128)(2,1)S(1)} async-done(((bf16[128,16,256]{0,2,1:T(8,128)(2,1)}), bf16[128,16,256]{0,2,1:T(8,128)(2,1)S(1)}, u32[]{:S(2)}, u32[]{:S(2)}) %all-to-all-start) | async-done | bytes 1048608 | tf_op jit(solution)/shard_map/all_to_all | solution.py:88
  61.9 0.7 copy.47
  62.6 0.6 reshape_reshape.3
  63.2 24.1 %all-gather.2.cloned.1.call-done = bf16[2048,256]{0,1:T(8,128)(2,1)} async-done(((bf16[128,256]{0,1:T(8,128)(2,1)}), bf16[2048,256]{0,1:T(8,128)(2,1)}) %all-gather.2.cloned.1.call-update) | async-done | bytes 1048592 | tf_op jit(solution)/shard_map/all_gather | solution.py:91
  87.2 2.1 %fusion.41 = (bf16[2048,128]{0,1:T(8,128)(2,1)S(1)}, bf16[2048,128]{0,1:T(8,128)(2,1)}) fusion(bf16[2048,256]{0,1:T(8,128)(2,1)} %all-gather.2.cloned.1.call-done), kind=kLoop, calls=%fused_computation.71 | loop fusion | bytes 2097152 | tf_op jit(solution)/shard_map/slice | solution.py:105
  89.3 0.3 copy.54
  89.6 1.3 copy.53
  90.9 0.2 convert_multiply_fusion.1
  91.1 1.6 %fusion.21 = f32[8,4,64,128]{3,2,1,0:T(8,128)S(1)} fusion(bf16[8,256,128,1]{2,1,3,0:T(8,128)(2,1)S(1)} %bitcast.72, f32[8,256,4,64]{1,0,3,2:T(8,128)S(1)} %convert_multiply_fusion.1), kind=kOutput, calls=%fused_computation.31 | convolution fusion | flops 805306368 | bytes 3670016 | tf_op jit(solution)/shard_map/cshp,csn->chpn/dot_general | solution.py:58
  92.8 1.6 %convolution_bitcast_fusion = f32[8,4,64,128]{3,0,2,1:T(8,128)S(1)} fusion(f32[8,4,64,128]{3,2,1,0:T(8,128)S(1)} %fusion.21, f32[4,8]{1,0:T(4,128)S(1)} %bitcast.76, f32[4,8]{1,0:T(4,128)S(1)} %subtract_bitcast_fusion, pred[8,8]{1,0:T(8,128)(4,1)S(1)} %iota_compare_fusion.1), kind=kOutput, calls=%fused_computation.36 | convolution fusion | flops 25166336 | bytes 2097472 | tf_op jit(solution)/shard_map/hcd,dhpn->chpn/dot_general | solution.py:62
  94.4 1.0 fusion.25
  95.4 0.4 fusion.43
  95.8 6.2 %bitcast_add_fusion = f32[8,256,4,64]{1,3,2,0:T(8,128)S(1)} fusion(f32[8,256,4,64]{1,3,2,0:T(8,128)S(1)} %fusion.25, f32[8,4,256]{2,1,0:T(4,128)S(1)} %copy.55, f32[8,256,256]{2,1,0:T(8,128)S(1)} %fusion.43, f32[8,4,256]{2,1,0:T(4,128)S(1)} %copy.51, pred[256,256]{1,0:T(8,128)(4,1)S(1)} %iota_compare_fusion, ...), kind=kOutput, calls=%fused_computation.28 | convolution fusion | flops 1620049920 | bytes 7503872 | tf_op jit(solution)/shard_map/chts,cshp->cthp/dot_general | solution.py:55
  102.0 2.8 %copy.61 = f32[8,256,4,64]{1,0,3,2:T(8,128)} copy(f32[8,256,4,64]{1,3,2,0:T(8,128)S(1)} %bitcast_add_fusion) | data formatting | bytes 4194304 | tf_op jit(solution)/shard_map/add | solution.py:66
  104.8 1.6 %reshape.121 = f32[16,128,256]{1,0,2:T(8,128)S(1)} reshape(f32[8,256,4,64]{1,0,3,2:T(8,128)} %copy.61) | data formatting | bytes 4194304 | tf_op jit(solution)/shard_map/reshape | solution.py:66
  106.4 1.7 %fusion.20 = bf16[16,128,256]{1,2,0:T(8,128)(2,1)} fusion(f32[16,128,256]{1,0,2:T(8,128)S(1)} %reshape.121, f32[256]{0:T(256)S(1)} %mul.156, bf16[128,16,256]{0,2,1:T(8,128)(2,1)S(1)} %all-to-all-done), kind=kLoop, calls=%fused_computation.30 | loop fusion | flops 2097152 | bytes 4195328 | tf_op jit(solution)/shard_map/convert_element_type | solution.py:110
  108.1 0.0 copy-start
  108.1 4.6 %all-to-all-start.2 = ((bf16[16,128,256]{1,2,0:T(8,128)(2,1)}), bf16[16,128,256]{1,2,0:T(8,128)(2,1)S(1)}, u32[]{:S(2)}, u32[]{:S(2)}) async-start(bf16[16,128,256]{1,2,0:T(8,128)(2,1)} %fusion.20), calls=%async_computation.2 | async-start | bytes 2097152 | tf_op jit(solution)/shard_map/all_to_all | solution.py:111
  112.7 0.0 copy-done
  112.8 0.0 copy-start.2
  112.8 0.7 copy.63
  113.4 23.4 %all-to-all-done.2 = bf16[16,128,256]{1,2,0:T(8,128)(2,1)S(1)} async-done(((bf16[16,128,256]{1,2,0:T(8,128)(2,1)}), bf16[16,128,256]{1,2,0:T(8,128)(2,1)S(1)}, u32[]{:S(2)}, u32[]{:S(2)}) %all-to-all-start.2) | async-done | bytes 1048608 | tf_op jit(solution)/shard_map/all_to_all | solution.py:111
  136.8 0.7 multiply_reduce_fusion
  137.5 0.0 copy-done.2
  137.5 0.9 multiply_convert_fusion.1
  138.4 1.3 copy.64
  (14 shorter events, 0.1 us)
Async XLA Ops:
  6.5 16.2 %copy-start.3 = (f32[64]{0:T(128)S(1)}, f32[64]{0:T(128)}, u32[]{:S(2)}) copy-start(f32[64]{0:T(128)} %param.14) | copy-start | bytes 772
  6.5 24.9 %all-to-all-start.1 = ((bf16[128,16,4]{0,2,1:T(4,128)(2,1)}), bf16[128,16,4]{0,2,1:T(4,128)(2,1)S(1)}, u32[]{:S(2)}, u32[]{:S(2)}) async-start(bf16[128,16,4]{0,2,1:T(4,128)(2,1)} %bitcast.77), calls=%async_computation.1 | async-start | bytes 32768 | tf_op jit(solution)/shard_map/all_to_all | solution.py:89
  15.0 72.3 %all-gather.2.cloned.1.call-start = ((), (), s32[]{:S(2)}) async-start(), calls=%async_computation.3 | async-start | bytes 1114112 | tf_op jit(solution)/shard_map/all_gather | solution.py:91
  15.9 6.9 %collective-permute-start = (bf16[3,4352]{1,0:T(4,128)(2,1)S(1)}, bf16[3,4352]{1,0:T(4,128)(2,1)S(1)}, u32[]{:S(2)}, u32[]{:S(2)}) collective-permute-start(bf16[3,4352]{1,0:T(4,128)(2,1)S(1)} %slice.49), channel_id=1, source_target_pairs={{0,2},{2,4},{4,6},{6,8},{8,10},{10,12},{12,14},{14,16},{16,18},{18... | collective-permute-start | bytes 78344 | tf_op jit(solution)/shard_map/ppermute | solution.py:15
  23.3 0.8 copy-start.1
  29.7 7.6 %copy-start.4 = (f32[64]{0:T(128)S(1)}, f32[64]{0:T(128)}, u32[]{:S(2)}) copy-start(f32[64]{0:T(128)} %param.15) | copy-start | bytes 772
  29.7 7.7 %copy-start.5 = (f32[64]{0:T(128)S(1)}, f32[64]{0:T(128)}, u32[]{:S(2)}) copy-start(f32[64]{0:T(128)} %param.16) | copy-start | bytes 772
  31.4 30.5 %all-to-all-start = ((bf16[128,16,256]{0,2,1:T(8,128)(2,1)}), bf16[128,16,256]{0,2,1:T(8,128)(2,1)S(1)}, u32[]{:S(2)}, u32[]{:S(2)}) async-start(bf16[128,16,256]{0,2,1:T(8,128)(2,1)} %bitcast), calls=%async_computation | async-start | bytes 2097152 | tf_op jit(solution)/shard_map/all_to_all | solution.py:88
  108.1 4.6 %copy-start = (bf16[128,4096]{1,0:T(8,128)(2,1)S(1)}, bf16[128,4096]{1,0:T(8,128)(2,1)}, u32[]{:S(2)}) copy-start(bf16[128,4096]{1,0:T(8,128)(2,1)} %param.10) | copy-start | bytes 3145732
  108.1 28.7 %all-to-all-start.2 = ((bf16[16,128,256]{1,2,0:T(8,128)(2,1)}), bf16[16,128,256]{1,2,0:T(8,128)(2,1)S(1)}, u32[]{:S(2)}, u32[]{:S(2)}) async-start(bf16[16,128,256]{1,2,0:T(8,128)(2,1)} %fusion.20), calls=%async_computation.2 | async-start | bytes 2097152 | tf_op jit(solution)/shard_map/all_to_all | solution.py:111
  112.8 24.8 %copy-start.2 = (f32[4096]{0:T(1024)S(1)}, f32[4096]{0:T(1024)}, u32[]{:S(2)}) copy-start(f32[4096]{0:T(1024)} %param.17) | copy-start | bytes 49156
Sparse Core Ops, SparseCore 0:
  31.5 55.6 all-gather.1
where the time goes:
time: 147 us
  waiting for transfers between devices  68.4 us (47%)
  starting transfers between devices  22.8 us (16%)
  local copies, waits for them, and re-layouts  18.1 us (12%)
  between operations  13.7 us (9%)
  other arithmetic  12.6 us (9%)
  matrix products  10.8 us (7%)
    all_gather x1, waiting for transfers between devices, shards(): lax.all_gather(activated[:, inner_width:], 'seq', axis=0, tiled=True)  24.1 us
    all_to_all x1, waiting for transfers between devices, shards(): lax.all_to_all(head_output, 'seq', split_axis=0, concat_axis=1, tiled=True)  23.4 us
    all_to_all x1, waiting for transfers between devices, shards(): lax.all_to_all(activated[:, :inner_width], 'seq', split_axis=1, concat_ax...  21 us
    all_to_all x1, starting transfers between devices, shards(): lax.all_to_all(step_input, 'seq', split_axis=1, concat_axis=0, tiled=True)  8.44 us
    dot_general x1, matrix products, dual_form(): jnp.einsum('chts,cshp->cthp', mixing, block_values, precision=highest)  6.18 us
    all_to_all x1, starting transfers between devices, shards(): lax.all_to_all(activated[:, :inner_width], 'seq', split_axis=1, concat_ax...  5.89 us
    convert_element_type x1, other arithmetic, convolve(): return jax.nn.silu(mixed).astype(jnp.bfloat16)  5.49 us
    all_to_all x1, starting transfers between devices, shards(): lax.all_to_all(head_output, 'seq', split_axis=0, concat_axis=1, tiled=True)  4.62 us
  transfers between devices with their start and end apart: 5, of which 3 were waited for; matrix products, arithmetic and copies ran while one was open for 12% of the time, Pallas kernels for 0%

commit v1 on v0

--- a/solution.py
+++ b/solution.py
@@ -85,7 +85,15 @@
     decay_rate = -jnp.exp(decay_log)
     activated = convolve(conv_input, conv_weight, convolution_bias)
     head_values, head_steps = (
-        lax.all_to_all(activated[:, :inner_width], "seq", split_axis=1, concat_axis=0, tiled=True),
+        jnp.concatenate(
+            lax.all_to_all(
+                jnp.stack(jnp.split(activated[:, :inner_width], lax.axis_size("seq"), axis=1)),
+                "seq",
+                0,
+                0,
+            ),
+            axis=0,
+        ),
         lax.all_to_all(step_input, "seq", split_axis=1, concat_axis=0, tiled=True),
     )
     shared = lax.all_gather(activated[:, inner_width:], "seq", axis=0, tiled=True)

time: 147 us -> 167 us (1.14)
  local copies, waits for them, and re-layouts: 18.1 us -> 30.8 us
  waiting for transfers between devices: 68.4 us -> 76 us
    all_gather x1, waiting for transfers between devices: 24.1 us -> 33.3 us  [shards(): lax.all_gather(activated[:, inner_width:], 'seq', axis=0, tiled=True)]
    unnamed x14 -> x28, local copies, waits for them, and re-layouts: 2.37 us -> 11 us
    reshape x1 -> x2, local copies, waits for them, and re-layouts: 1.63 us -> 7.32 us  [dual_form(): result = (inside + outside).reshape(row_count, head_count, head_width)]
    convert_element_type x1, other arithmetic: 5.49 us -> 1.42 us  [convolve(): return jax.nn.silu(mixed).astype(jnp.bfloat16)]
    add x1 -> x0, local copies, waits for them, and re-layouts: 2.79 us -> none  [dual_form(): result = (inside + outside).reshape(row_count, head_count, head_width)]
    all_to_all x1, starting transfers between devices: 8.44 us -> 5.95 us  [shards(): lax.all_to_all(step_input, 'seq', split_axis=1, concat_axis=0, tiled=True)]
    slice x3 -> x1, local copies, waits for them, and re-layouts: 2.51 us -> 0.16 us  [the longest x1 1.31 us: shards(): shared_rows[:, STATE:]]
    convert_element_type x0 -> x1, local copies, waits for them, and re-layouts: none -> 1.91 us  [gated_norm(): mixed_out.astype(jnp.float32) * jax.nn.silu(gate_input.astype(jnp.float32))]
  transfers between devices with their start and end apart: 5 -> 5, of which waited for: 3 -> 3; matrix products, arithmetic and copies ran while one was open for 12% -> 14% of each run, Pallas kernels for 0% -> 0%
where the time goes in v1:
time: 167 us; the launch traced here: 166 us
  waiting for transfers between devices  76 us (46%)
  local copies, waits for them, and re-layouts  30.8 us (18%)
  starting transfers between devices  22.3 us (13%)
  between operations  13.7 us (8%)
  other arithmetic  12.6 us (8%)
  matrix products  10.9 us (7%)
    all_gather x1, waiting for transfers between devices, shards(): lax.all_gather(activated[:, inner_width:], 'seq', axis=0, tiled=True)  33.3 us
    all_to_all x1, waiting for transfers between devices, shards(): lax.all_to_all(head_output, 'seq', split_axis=0, concat_axis=1, tiled=True)  22.6 us
    all_to_all x1, waiting for transfers between devices, shards(): lax.all_to_all(jnp.stack(jnp.split(activated[:, :inner_width], lax.axis_s...  20.1 us
    unnamed x28, local copies, waits for them, and re-layouts  11 us
    reshape x2, local copies, waits for them, and re-layouts, dual_form(): result = (inside + outside).reshape(row_count, head_count, head_width)  7.32 us
    all_to_all x1, starting transfers between devices, shards(): lax.all_to_all(jnp.stack(jnp.split(activated[:, :inner_width], lax.axis_s...  6.91 us
    dot_general x1, matrix products, dual_form(): jnp.einsum('chts,cshp->cthp', mixing, block_values, precision=highest)  6.18 us
    all_to_all x1, starting transfers between devices, shards(): lax.all_to_all(step_input, 'seq', split_axis=1, concat_axis=0, tiled=True)  5.95 us
  transfers between devices with their start and end apart: 5, of which 3 were waited for; matrix products, arithmetic and copies ran while one was open for 14% of the time, Pallas kernels for 0%

profile of v1, /device:TPU:0, one launch (start us, length us, event | category | flops | bytes accessed | tf_op | source)
XLA Modules:
  0.0 166.3 jit_solution(6979618665947772171)
XLA Ops:
  6.5 0.9 slice.63
  7.4 4.8 %collective-permute-start = (bf16[3,4352]{1,0:T(4,128)(2,1)S(1)}, bf16[3,4352]{1,0:T(4,128)(2,1)S(1)}, u32[]{:S(2)}, u32[]{:S(2)}) collective-permute-start(bf16[3,4352]{1,0:T(4,128)(2,1)S(1)} %slice.63), channel_id=1, source_target_pairs={{0,2},{2,4},{4,6},{6,8},{8,10},{10,12},{12,14},{14,16},{16,18},{18... | collective-permute-start | bytes 78344 | tf_op jit(solution)/shard_map/ppermute | solution.py:15
  12.3 6.0 %all-to-all-start.1 = ((bf16[128,16,4]{0,2,1:T(4,128)(2,1)}), bf16[128,16,4]{0,2,1:T(4,128)(2,1)S(1)}, u32[]{:S(2)}, u32[]{:S(2)}) async-start(bf16[128,16,4]{0,2,1:T(4,128)(2,1)} %bitcast.133), calls=%async_computation.1 | async-start | bytes 32768 | tf_op jit(solution)/shard_map/all_to_all | solution.py:97
  18.3 1.2 slice_reduce_fusion.4
  19.5 0.7 dynamic_slice.9
  20.2 1.5 maximum_convert_fusion
  21.7 1.4 multiply_convert_fusion
  23.2 0.0 copy-start.5
  23.2 0.6 fusion.43
  23.8 0.6 fusion.42
  24.5 0.6 fusion.41
  25.1 0.6 fusion.40
  25.7 0.6 fusion.39
  26.4 0.6 fusion.38
  27.0 0.6 fusion.37
  27.6 0.6 fusion.36
  28.3 0.6 fusion.35
  28.9 0.6 fusion.34
  29.5 0.6 fusion.33
  30.2 0.6 fusion.32
  30.8 0.6 fusion.31
  31.4 0.6 fusion.30
  32.1 0.6 fusion.29
  32.7 0.6 fusion.28
  33.3 6.9 %all-to-all-start = ((bf16[16,128,256]{2,1,0:T(8,128)(2,1)}), bf16[16,128,256]{2,1,0:T(8,128)(2,1)S(1)}, u32[]{:S(2)}, u32[]{:S(2)}) async-start(bf16[16,128,256]{2,1,0:T(8,128)(2,1)} %fusion.28), calls=%async_computation | async-start | bytes 2097152 | tf_op jit(solution)/shard_map/all_to_all | solution.py:89
  40.3 0.0 all-gather.2.cloned.1.call-start
  40.3 0.1 dynamic_slice.10
  40.4 0.1 dynamic_slice.11
  40.5 0.1 mul.155
  40.6 0.1 mul.156
  40.7 0.6 slice.83
  41.3 0.0 all-gather.2.cloned.1.call-update
  41.4 0.1 multiply_bitcast_fusion
  41.5 2.5 %reduce-window.6 = f32[8,4,2,128]{3,0,1,2:T(8,128)S(1)} reduce-window(f32[8,4,2,128]{3,0,1,2:T(8,128)S(1)} %copy.63, f32[]{:T(128)} %constant.30.clone.1), window={size=1x1x1x128 pad=0_0x0_0x0_0x127_0}, to_apply=%region_0.1 | reduce-window | flops 1040384 | bytes 65540 | tf_op jit(solution)/shard_map/reduce-window
  43.9 0.2 slice_reduce_fusion
  44.1 0.1 copy_bitcast_fusion
  44.2 0.2 slice_reduce_fusion.5
  44.4 0.2 reduce_window_sum.36
  44.5 0.1 fusion.55
  44.7 20.1 %all-to-all-done = bf16[16,128,256]{2,1,0:T(8,128)(2,1)S(1)} async-done(((bf16[16,128,256]{2,1,0:T(8,128)(2,1)}), bf16[16,128,256]{2,1,0:T(8,128)(2,1)S(1)}, u32[]{:S(2)}, u32[]{:S(2)}) %all-to-all-start) | async-done | bytes 1048608 | tf_op jit(solution)/shard_map/all_to_all | solution.py:89
  64.8 1.1 copy.61
  65.9 1.2 reshape_reshape.3
  67.1 1.4 convert_multiply_fusion.1
  68.5 33.3 %all-gather.2.cloned.1.call-done = bf16[2048,256]{1,0:T(8,128)(2,1)} async-done(((bf16[128,256]{1,0:T(8,128)(2,1)}), bf16[2048,256]{1,0:T(8,128)(2,1)}) %all-gather.2.cloned.1.call-update) | async-done | bytes 1048592 | tf_op jit(solution)/shard_map/all_gather | solution.py:99
  101.8 1.3 fusion.56
  103.0 1.7 fusion.20
  104.7 1.6 convolution_bitcast_fusion
  106.3 1.0 fusion.24
  107.3 0.0 copy-start
  107.3 0.4 fusion.58
  107.7 0.8 copy-done
  108.5 6.2 %bitcast_add_fusion = f32[8,256,4,64]{1,3,2,0:T(8,128)S(1)} fusion(f32[8,256,4,64]{1,3,2,0:T(8,128)S(1)} %fusion.24, f32[8,4,256]{2,1,0:T(4,128)S(1)} %copy.67, f32[8,256,256]{2,1,0:T(8,128)S(1)} %fusion.58, f32[8,4,256]{2,1,0:T(4,128)S(1)} %copy.65, pred[256,256]{1,0:T(8,128)(4,1)S(1)} %iota_compare_fusion, bf16[8,256,4,64]{1,0,3,2:T(8,128)(2,1)S(1)} %copy-done, ...), kind=kOutput, calls=%fused_computation.27 | convolution fusion | flops 1620049920 | bytes 7503872 | tf_op jit(solution)/shard_map/chts,cshp->cthp/dot_general | solution.py:55
  114.7 3.2 %copy.81 = f32[8,256,4,64]{3,2,1,0:T(4,128)} copy(f32[8,256,4,64]{1,3,2,0:T(8,128)S(1)} %bitcast_add_fusion) | data formatting | bytes 4194304 | tf_op jit(solution)/shard_map/reshape | solution.py:66
  117.9 4.2 %reshape.125 = f32[16,128,256]{2,1,0:T(8,128)S(1)} reshape(f32[8,256,4,64]{3,2,1,0:T(4,128)} %copy.81) | data formatting | bytes 4194304 | tf_op jit(solution)/shard_map/reshape | solution.py:66
  122.0 1.3 add_convert_fusion
  123.3 4.6 %all-to-all-start.2 = ((bf16[16,128,256]{2,1,0:T(8,128)(2,1)}), bf16[16,128,256]{2,1,0:T(8,128)(2,1)S(1)}, u32[]{:S(2)}, u32[]{:S(2)}) async-start(bf16[16,128,256]{2,1,0:T(8,128)(2,1)} %add_convert_fusion), calls=%async_computation.2 | async-start | bytes 2097152 | tf_op jit(solution)/shard_map/all_to_all | solution.py:119
  127.9 0.7 copy.76
  128.6 22.6 %all-to-all-done.2 = bf16[16,128,256]{2,1,0:T(8,128)(2,1)S(1)} async-done(((bf16[16,128,256]{2,1,0:T(8,128)(2,1)}), bf16[16,128,256]{2,1,0:T(8,128)(2,1)S(1)}, u32[]{:S(2)}, u32[]{:S(2)}) %all-to-all-start.2) | async-done | bytes 1048608 | tf_op jit(solution)/shard_map/all_to_all | solution.py:119
  151.2 1.6 convert_bitcast_fusion
  152.8 1.9 %copy.75 = f32[128,16,256]{0,2,1:T(8,128)S(1)} copy(f32[128,16,256]{2,0,1:T(8,128)} %convert_bitcast_fusion) | data formatting | bytes 4194304 | tf_op jit(solution)/shard_map/convert_element_type | solution.py:19
  154.7 0.0 copy-start.3
  154.7 0.7 multiply_reduce_fusion
  155.5 1.7 %multiply_convert_fusion.1 = bf16[128,4096]{0,1:T(8,128)(2,1)} fusion(f32[4096]{0:T(1024)S(1)} %copy-done.3, f32[128]{0:T(128)S(1)} %add_rsqrt_fusion, bf16[128,4096]{0,1:T(8,128)(2,1)S(1)} %copy.76, f32[128,16,256]{0,2,1:T(8,128)S(1)} %copy.75), kind=kLoop, calls=%fused_computation.31 | loop fusion | flops 4718592 | bytes 4211200 | tf_op jit(solution)/shard_map/convert_element_type | solution.py:21
  157.2 2.3 %copy.77 = bf16[128,4096]{1,0:T(8,128)(2,1)} copy(bf16[128,4096]{0,1:T(8,128)(2,1)} %multiply_convert_fusion.1) | data formatting | bytes 2097152 | tf_op jit(solution)/shard_map/convert_element_type | solution.py:21
  (24 shorter events, 0.2 us)
Async XLA Ops:
  6.5 15.2 %copy-start.2 = (f32[4352]{0:T(1024)S(1)}, f32[4352]{0:T(1024)}, u32[]{:S(2)}) copy-start(f32[4352]{0:T(1024)} %param.13) | copy-start | bytes 52228
  7.4 12.8 %collective-permute-start = (bf16[3,4352]{1,0:T(4,128)(2,1)S(1)}, bf16[3,4352]{1,0:T(4,128)(2,1)S(1)}, u32[]{:S(2)}, u32[]{:S(2)}) collective-permute-start(bf16[3,4352]{1,0:T(4,128)(2,1)S(1)} %slice.63), channel_id=1, source_target_pairs={{0,2},{2,4},{4,6},{6,8},{8,10},{10,12},{12,14},{14,16},{16,18},{18... | collective-permute-start | bytes 78344 | tf_op jit(solution)/shard_map/ppermute | solution.py:15
  12.3 21.0 %all-to-all-start.1 = ((bf16[128,16,4]{0,2,1:T(4,128)(2,1)}), bf16[128,16,4]{0,2,1:T(4,128)(2,1)S(1)}, u32[]{:S(2)}, u32[]{:S(2)}) async-start(bf16[128,16,4]{0,2,1:T(4,128)(2,1)} %bitcast.133), calls=%async_computation.1 | async-start | bytes 32768 | tf_op jit(solution)/shard_map/all_to_all | solution.py:97
  23.2 17.1 %copy-start.4 = (f32[64]{0:T(128)S(1)}, f32[64]{0:T(128)}, u32[]{:S(2)}) copy-start(f32[64]{0:T(128)} %param.15) | copy-start | bytes 772
  23.2 17.2 %copy-start.5 = (f32[64]{0:T(128)S(1)}, f32[64]{0:T(128)}, u32[]{:S(2)}) copy-start(f32[64]{0:T(128)} %param.16) | copy-start | bytes 772
  33.3 31.5 %all-to-all-start = ((bf16[16,128,256]{2,1,0:T(8,128)(2,1)}), bf16[16,128,256]{2,1,0:T(8,128)(2,1)S(1)}, u32[]{:S(2)}, u32[]{:S(2)}) async-start(bf16[16,128,256]{2,1,0:T(8,128)(2,1)} %fusion.28), calls=%async_computation | async-start | bytes 2097152 | tf_op jit(solution)/shard_map/all_to_all | solution.py:89
  40.3 61.5 %all-gather.2.cloned.1.call-start = ((), (), s32[]{:S(2)}) async-start(), calls=%async_computation.3 | async-start | bytes 1114112 | tf_op jit(solution)/shard_map/all_gather | solution.py:99
  107.3 1.2 copy-start
  123.3 4.6 %copy-start.1 = (bf16[128,4096]{1,0:T(8,128)(2,1)S(1)}, bf16[128,4096]{1,0:T(8,128)(2,1)}, u32[]{:S(2)}) copy-start(bf16[128,4096]{1,0:T(8,128)(2,1)} %param.10) | copy-start | bytes 3145732
  123.3 27.9 %all-to-all-start.2 = ((bf16[16,128,256]{2,1,0:T(8,128)(2,1)}), bf16[16,128,256]{2,1,0:T(8,128)(2,1)S(1)}, u32[]{:S(2)}, u32[]{:S(2)}) async-start(bf16[16,128,256]{2,1,0:T(8,128)(2,1)} %add_convert_fusion), calls=%async_computation.2 | async-start | bytes 2097152 | tf_op jit(solution)/shard_map/all_to_all | solution.py:119
  154.7 0.8 copy-start.3
Sparse Core Ops, SparseCore 0:
  43.9 57.8 all-gather.1
